TPU v7x, 128 devices: a whole 4x4x4 slice. The times are simulated.
128 devices in a mesh: wide: 8 (over y, core), narrow: 16 (over x, z).
Axes of the slice: x: 4, y: 4, z: 4, core: 2. Of those that a mesh axis runs over, the one named last changes fastest.
Arguments:
- slip: bfloat16 [2, 524288], P(None, ('wide', 'narrow')), may hold values from -6 to 6
- effect_stress: float32 [2, 524288], P(None, ('wide', 'narrow')), may hold values from 0.5 to 4
- home_blocks: int32 [2048], P(('wide', 'narrow')), may hold values from 0 to 2047, as said below
- far_list: int32 [3, 49152], P(None, ('wide', 'narrow')), may hold values from 0 to 2047, as said below
- u_factor: bfloat16 [49152, 32, 256], P(('wide', 'narrow')), may hold values from -0.1875 to 0.1875
- v_factor: bfloat16 [49152, 32, 256], P(('wide', 'narrow')), may hold values from -0.1875 to 0.1875
- near_list: int32 [3, 8192], P(None, ('wide', 'narrow')), may hold values from 0 to 2047, as said below
- near_block: bfloat16 [8192, 256, 256], P(('wide', 'narrow')), may hold values from -0.1875 to 0.1875
Outputs:
- stress_first: float32 [2, 524288], P(None, ('wide', 'narrow'))
- stress_second: float32 [2, 524288], P(None, ('wide', 'narrow'))
Inputs may be any that keep to these rules, and one draw needn't show every extreme that they name: `home_blocks`: a permutation of the 2048 blocks. `far_list`: entry e lies on device e // 384; its row block is one that this device stores (among its 16 positions of home_blocks); its column block may be any block. Among one device's entries at most 4 have column blocks stored by any one device, and on every device exactly 4 do for some storing device. The slots of one device are a permutation of 0 to 383. `near_list`: entry n lies on device n // 64; its row and column blocks are both stored by that device. The slots of one device are a permutation of 0 to 63.
All inputs are finite; a program needn't handle non-finite values.
Results may differ from a plain program's by a relative error of at most 0.0034.
Values may be sent and summed in bfloat16 or wider, within the bound.
A program may use at most 128 MiB of HBM per device.

v0:
```python
import jax
import jax.numpy as jnp
from jax import lax
from jax.sharding import PartitionSpec as P


def inverse_order(slot_order):
    count = slot_order.shape[0]
    return jnp.zeros((count,), jnp.int32).at[slot_order].set(jnp.arange(count, dtype=jnp.int32))


def local(slip, effect_stress, home_blocks, far_list, u_factor, v_factor, near_list, near_block):
    devices = lax.axis_size(("wide", "narrow"))
    nb_dev = home_blocks.shape[0]
    block_size = slip.shape[1] // nb_dev
    adm_count = far_list.shape[1]
    capacity = max(2, adm_count // devices + 1)
    highest = lax.Precision.HIGHEST
    home_all = lax.all_gather(home_blocks, ("wide", "narrow"), axis=0, tiled=True)
    places = jnp.arange(home_all.shape[0], dtype=jnp.int32)
    where_col = jnp.sum(
        jnp.where(home_all[None, :] == far_list[1][:, None], places[None, :], 0), axis=1
    )
    owner_device = where_col // nb_dev
    col_slot = where_col % nb_dev
    owner_hot = (owner_device[:, None] == jnp.arange(devices, dtype=jnp.int32)[None, :]).astype(
        jnp.int32
    )
    earlier = jnp.cumsum(owner_hot, axis=0) - owner_hot
    rank_slot = jnp.sum(earlier * owner_hot, axis=1)
    destination = owner_device * capacity + rank_slot
    request = jnp.full((devices * capacity,), -1, jnp.int32).at[destination].set(col_slot)
    request = request.reshape(devices, capacity)
    incoming = lax.all_to_all(request, ("wide", "narrow"), split_axis=0, concat_axis=0, tiled=True)
    factor_entry = inverse_order(far_list[2])
    dest_factor = destination[factor_entry]
    row_hot = (far_list[0][factor_entry][:, None] == home_blocks[None, :]).astype(jnp.float32)
    row_hot_bf = row_hot.astype(jnp.bfloat16)
    near_entry = inverse_order(near_list[2])
    near_rows = near_list[0][near_entry]
    near_cols = near_list[1][near_entry]
    near_row_hot = (near_rows[:, None] == home_blocks[None, :]).astype(jnp.float32)
    near_col_hot = (near_cols[:, None] == home_blocks[None, :]).astype(jnp.bfloat16)
    incoming_flat = incoming.reshape(-1)
    incoming_hot = (incoming_flat[:, None] == jnp.arange(nb_dev, dtype=jnp.int32)[None, :]).astype(
        jnp.float32
    )
    incoming_valid = (incoming >= 0).astype(jnp.bfloat16)[:, :, None, None]
    wanted = jnp.maximum(incoming, 0)

    def apply_kernel(rates):
        xblocks = rates.reshape(2, nb_dev, block_size).transpose(1, 0, 2)
        reply_blocks = xblocks[wanted] * incoming_valid
        arrived = lax.all_to_all(
            reply_blocks, ("wide", "narrow"), split_axis=0, concat_axis=0, tiled=True
        )
        col_rates = arrived.reshape(devices * capacity, 2, block_size)[dest_factor]
        reduced = jnp.einsum(
            "erb,ecb->ecr", v_factor, col_rates, preferred_element_type=jnp.float32
        ).astype(jnp.bfloat16)
        forward_terms = jnp.einsum(
            "erb,ecr->ecb", u_factor, reduced, preferred_element_type=jnp.float32
        )
        row_rates = jnp.einsum(
            "es,scb->ecb", row_hot_bf, xblocks, preferred_element_type=jnp.float32
        ).astype(jnp.bfloat16)
        projected = jnp.einsum(
            "erb,ecb->ecr", u_factor, row_rates, preferred_element_type=jnp.float32
        ).astype(jnp.bfloat16)
        back_terms = jnp.einsum(
            "erb,ecr->ecb", v_factor, projected, preferred_element_type=jnp.float32
        )
        near_rates = jnp.einsum(
            "ns,scb->ncb", near_col_hot, xblocks, preferred_element_type=jnp.float32
        ).astype(jnp.bfloat16)
        near_terms = jnp.einsum(
            "nij,ncj->nci", near_block, near_rates, preferred_element_type=jnp.float32
        )
        accumulated = jnp.einsum("es,ecb->scb", row_hot, forward_terms, precision=highest)
        accumulated = accumulated + jnp.einsum(
            "ns,ncb->scb", near_row_hot, near_terms, precision=highest
        )
        outgoing = (
            jnp.zeros((devices * capacity, 2, block_size), jnp.float32)
            .at[dest_factor]
            .set(back_terms)
        )
        outgoing = outgoing.reshape(devices, capacity, 2, block_size)
        returned = lax.all_to_all(
            outgoing, ("wide", "narrow"), split_axis=0, concat_axis=0, tiled=True
        )
        returned = returned.reshape(devices * capacity, 2, block_size)
        accumulated = accumulated + jnp.einsum(
            "ks,kcb->scb", incoming_hot, returned, precision=highest
        )
        return accumulated.transpose(1, 0, 2).reshape(2, nb_dev * block_size)

    first_stress = apply_kernel(slip)
    mid_rate = (slip.astype(jnp.float32) * jnp.exp(jnp.tanh(first_stress / effect_stress))).astype(
        jnp.bfloat16
    )
    second_stress = apply_kernel(mid_rate)
    return (first_stress, second_stress)


def solution(mesh):
    in_specs = (
        P(None, ("wide", "narrow")),
        P(None, ("wide", "narrow")),
        P(("wide", "narrow")),
        P(None, ("wide", "narrow")),
        P(("wide", "narrow"), None, None),
        P(("wide", "narrow"), None, None),
        P(None, ("wide", "narrow")),
        P(("wide", "narrow"), None, None),
    )
    out_specs = (P(None, ("wide", "narrow")), P(None, ("wide", "narrow")))
    return jax.shard_map(local, mesh=mesh, in_specs=in_specs, out_specs=out_specs, check_vma=False)
```

profile of v0, /device:TPU:1, one launch (start us, length us, event | category | flops | bytes accessed | tf_op | source)
XLA Modules:
  0.0 233.7 jit_solution(8595274305735432068)
XLA Ops:
  0.7 0.8 slice_reduce_fusion.1
  1.5 0.9 dynamic-update-slice
  2.3 68.7 %all-reduce = s32[2048]{0:T(1024)S(1)} all-reduce(s32[2048]{0:T(1024)S(1)} %dynamic-update-slice), channel_id=1, replica_groups=mesh['wide'=8,'narrow'=16] {'wide','narrow'}, use_global_device_ids=true, to_apply=%add | all-reduce | flops 2048 | bytes 16384
  72.3 2.9 %scatter_custom_fusion.1 = s32[512]{0:T(512)S(1)} fusion(s32[384]{0:T(512)S(1)} %fusion.67, s32[384]{0:T(512)S(1)} %get-tuple-element.6, s32[]{:T(128)} %constant.40.clone.1), kind=kCustom, calls=%fused_computation.132 | custom fusion | bytes 2052 | tf_op jit(solution)/shard_map/scatter | solution.py:32
  76.0 4.7 %all-to-all-start = ((s32[128,1,4]{2,1,0:T(1,128)}), s32[128,1,4]{2,1,0:T(1,128)S(1)}, u32[]{:S(2)}, u32[]{:S(2)}) async-start(s32[128,1,4]{2,1,0:T(1,128)} %bitcast.8), calls=%async_computation | async-start | bytes 131072 | tf_op jit(solution)/shard_map/all_to_all | solution.py:34
  83.6 3.1 %scatter_custom_fusion = s32[384]{0:T(512)S(1)} fusion(s32[384]{0:T(512)S(1)} %fusion.66, s32[384]{0:T(512)S(1)} %iota.22, s32[]{:T(128)} %constant.38.clone.1), kind=kCustom, calls=%fused_computation.135 | custom fusion | bytes 1540 | tf_op jit(solution)/shard_map/scatter | solution.py:9
  86.8 2.8 %gather_fusion = s32[384]{0:T(512)S(1)} fusion(s32[384]{0:T(512)S(1)} %get-tuple-element.2, s32[1024]{0:T(1024)S(1)} %pad_clamp_fusion.3), kind=kCustom, calls=%fused_computation | custom fusion | bytes 4608 | tf_op jit(solution)/shard_map/gather | solution.py:37
  89.6 2.8 %gather_fusion.2 = s32[384]{0:T(512)S(1)} fusion(s32[384]{0:T(512)S(1)} %multiply_add_fusion, s32[1024]{0:T(1024)S(1)} %pad_clamp_fusion.3), kind=kCustom, calls=%fused_computation.2 | custom fusion | bytes 4608 | tf_op jit(solution)/shard_map/gather | solution.py:36
  93.8 7.1 %fusion.3 = f32[384,2,256]{2,1,0:T(2,128)S(1)} fusion(bf16[384,32,256]{2,1,0:T(8,128)(2,1)} %param.13, bf16[384,32,256]{2,1,0:T(8,128)(2,1)} %param.12, bf16[384,2,256]{2,0,1:T(8,128)(2,1)S(1)} %convolution_convert_fusion.1), kind=kOutput, calls=%fused_computation.29 | convolution fusion | flops 25190400 | bytes 13762560 | tf_op jit(solution)/shard_map/erb,ecr->ecb/dot_general | solution.py:70
  102.0 12.0 %scatter_fusion = f32[512,2,256]{2,1,0:T(2,128)S(1)} fusion(f32[512,2,256]{2,1,0:T(2,128)S(1)} %broadcast.220.clone, s32[384]{0:T(512)S(1)} %fusion.68, f32[384,2,256]{2,1,0:T(2,128)S(1)} %fusion.3), kind=kCustom, calls=%fused_computation.11 | custom fusion | bytes 2360832 | tf_op jit(solution)/shard_map/scatter | solution.py:86
  114.0 1.3 copy.88
  115.8 2.6 %gather_fusion.1 = bf16[512,2,256]{2,1,0:T(2,128)(2,1)S(1)} fusion(bf16[16,2,256]{2,1,0:T(2,128)(2,1)S(1)} %bitcast.109, s32[1024]{0:T(1024)S(1)} %pad_clamp_fusion.2), kind=kCustom, calls=%fused_computation.1 | custom fusion | bytes 1050624 | tf_op jit(solution)/shard_map/gather | solution.py:53
  118.3 1.4 broadcast_multiply_fusion.1
  119.8 9.8 %all-to-all-start.1 = ((bf16[128,4,2,256]{3,2,1,0:T(2,128)(2,1)}), bf16[128,4,2,256]{3,2,1,0:T(2,128)(2,1)S(1)}, u32[]{:S(2)}, u32[]{:S(2)}) async-start(bf16[128,4,2,256]{3,2,1,0:T(2,128)(2,1)} %broadcast_multiply_fusion.1), calls=%async_computation.1 | async-start | bytes 1048576 | tf_op jit(solution)/shard_map/all_to_all | solution.py:54
  129.6 5.6 %fusion.23 = f32[64,2,256]{2,1,0:T(2,128)S(1)} fusion(bf16[64,256,256]{2,1,0:T(8,128)(2,1)} %param.15, bf16[64,2,256]{2,0,1:T(8,128)(2,1)S(1)} %convolution_convert_fusion.7), kind=kOutput, calls=%fused_computation.53 | convolution fusion | flops 16777216 | bytes 8585216 | tf_op jit(solution)/shard_map/nij,ncj->nci/dot_general | solution.py:76
  135.7 0.8 reduce.13
  136.6 6.3 %all-to-all-done.1 = bf16[128,4,2,256]{3,2,1,0:T(2,128)(2,1)S(1)} async-done(((bf16[128,4,2,256]{3,2,1,0:T(2,128)(2,1)}), bf16[128,4,2,256]{3,2,1,0:T(2,128)(2,1)S(1)}, u32[]{:S(2)}, u32[]{:S(2)}) %all-to-all-start.1) | async-done | bytes 524320 | tf_op jit(solution)/shard_map/all_to_all | solution.py:54
  143.0 4.7 %all-to-all-start.2 = ((f32[128,4,2,256]{3,1,2,0:T(4,128)}), f32[128,4,2,256]{3,1,2,0:T(4,128)S(1)}, u32[]{:S(2)}, u32[]{:S(2)}) async-start(f32[128,4,2,256]{3,1,2,0:T(4,128)} %copy.88), calls=%async_computation.2 | async-start | bytes 2097152 | tf_op jit(solution)/shard_map/all_to_all | solution.py:89
  147.7 2.5 %gather_fusion.3 = bf16[384,2,256]{2,1,0:T(2,128)(2,1)S(1)} fusion(bf16[512,2,256]{2,1,0:T(2,128)(2,1)S(1)} %bitcast.118, s32[1024]{0:T(1024)S(1)} %pad_clamp_fusion.1), kind=kCustom, calls=%fused_computation.3 | custom fusion | bytes 787968 | tf_op jit(solution)/shard_map/gather | solution.py:57
  150.2 7.1 %fusion.2 = f32[384,2,256]{2,1,0:T(2,128)S(1)} fusion(bf16[384,32,256]{2,1,0:T(8,128)(2,1)} %param.12, bf16[384,2,256]{2,1,0:T(2,128)(2,1)S(1)} %gather_fusion.3, bf16[384,32,256]{2,1,0:T(8,128)(2,1)} %param.13), kind=kOutput, calls=%fused_computation.28 | convolution fusion | flops 25190400 | bytes 13762560 | tf_op jit(solution)/shard_map/erb,ecr->ecb/dot_general | solution.py:61
  157.9 8.5 %all-to-all-done.2 = f32[128,4,2,256]{3,1,2,0:T(4,128)S(1)} async-done(((f32[128,4,2,256]{3,1,2,0:T(4,128)}), f32[128,4,2,256]{3,1,2,0:T(4,128)S(1)}, u32[]{:S(2)}, u32[]{:S(2)}) %all-to-all-start.2) | async-done | bytes 1048608 | tf_op jit(solution)/shard_map/all_to_all | solution.py:89
  168.2 2.6 %gather_fusion.6 = bf16[512,2,256]{2,1,0:T(2,128)(2,1)S(1)} fusion(bf16[16,2,256]{2,1,0:T(2,128)(2,1)S(1)} %bitcast.112, s32[1024]{0:T(1024)S(1)} %pad_clamp_fusion.2), kind=kCustom, calls=%fused_computation.6 | custom fusion | bytes 1050624 | tf_op jit(solution)/shard_map/gather | solution.py:53
  170.8 7.2 %fusion.5 = f32[384,2,256]{2,1,0:T(2,128)S(1)} fusion(bf16[384,32,256]{2,1,0:T(8,128)(2,1)} %param.13, bf16[384,32,256]{2,1,0:T(8,128)(2,1)} %param.12, bf16[384,2,256]{2,0,1:T(8,128)(2,1)S(1)} %convolution_convert_fusion), kind=kOutput, calls=%fused_computation.31 | convolution fusion | flops 25190400 | bytes 13762560 | tf_op jit(solution)/shard_map/erb,ecr->ecb/dot_general | solution.py:70
  178.0 1.4 broadcast_multiply_fusion
  179.4 4.9 %all-to-all-start.3 = ((bf16[128,4,2,256]{3,2,1,0:T(2,128)(2,1)}), bf16[128,4,2,256]{3,2,1,0:T(2,128)(2,1)S(1)}, u32[]{:S(2)}, u32[]{:S(2)}) async-start(bf16[128,4,2,256]{3,2,1,0:T(2,128)(2,1)} %broadcast_multiply_fusion), calls=%async_computation.3 | async-start | bytes 1048576 | tf_op jit(solution)/shard_map/all_to_all | solution.py:54
  184.6 12.0 %scatter_fusion.1 = f32[512,2,256]{2,1,0:T(2,128)S(1)} fusion(f32[512,2,256]{2,1,0:T(2,128)S(1)} %broadcast.220, s32[384]{0:T(512)S(1)} %fusion.68, f32[384,2,256]{2,1,0:T(2,128)S(1)} %fusion.5), kind=kCustom, calls=%fused_computation.12 | custom fusion | bytes 2360832 | tf_op jit(solution)/shard_map/scatter | solution.py:86
  196.6 1.3 copy.96
  197.9 5.6 %fusion.21 = f32[64,2,256]{2,1,0:T(2,128)S(1)} fusion(bf16[64,256,256]{2,1,0:T(8,128)(2,1)} %param.15, bf16[64,2,256]{2,0,1:T(8,128)(2,1)S(1)} %convolution_convert_fusion.6), kind=kOutput, calls=%fused_computation.51 | convolution fusion | flops 16777216 | bytes 8585216 | tf_op jit(solution)/shard_map/nij,ncj->nci/dot_general | solution.py:76
  203.5 9.9 %all-to-all-start.4 = ((f32[128,4,2,256]{3,1,2,0:T(4,128)}), f32[128,4,2,256]{3,1,2,0:T(4,128)S(1)}, u32[]{:S(2)}, u32[]{:S(2)}) async-start(f32[128,4,2,256]{3,1,2,0:T(4,128)} %copy.96), calls=%async_computation.4 | async-start | bytes 2097152 | tf_op jit(solution)/shard_map/all_to_all | solution.py:89
  213.4 2.5 %gather_fusion.7 = bf16[384,2,256]{2,1,0:T(2,128)(2,1)S(1)} fusion(bf16[512,2,256]{2,1,0:T(2,128)(2,1)S(1)} %bitcast.117, s32[1024]{0:T(1024)S(1)} %pad_clamp_fusion.1), kind=kCustom, calls=%fused_computation.7 | custom fusion | bytes 787968 | tf_op jit(solution)/shard_map/gather | solution.py:57
  215.9 7.1 %fusion.4 = f32[384,2,256]{2,1,0:T(2,128)S(1)} fusion(bf16[384,32,256]{2,1,0:T(8,128)(2,1)} %param.12, bf16[384,2,256]{2,1,0:T(2,128)(2,1)S(1)} %gather_fusion.7, bf16[384,32,256]{2,1,0:T(8,128)(2,1)} %param.13), kind=kOutput, calls=%fused_computation.30 | convolution fusion | flops 25190400 | bytes 13762560 | tf_op jit(solution)/shard_map/erb,ecr->ecb/dot_general | solution.py:61
  223.7 8.4 %all-to-all-done.4 = f32[128,4,2,256]{3,1,2,0:T(4,128)S(1)} async-done(((f32[128,4,2,256]{3,1,2,0:T(4,128)}), f32[128,4,2,256]{3,1,2,0:T(4,128)S(1)}, u32[]{:S(2)}, u32[]{:S(2)}) %all-to-all-start.4) | async-done | bytes 1048608 | tf_op jit(solution)/shard_map/all_to_all | solution.py:89
  (66 shorter events, 13.3 us)
Async XLA Ops:
  0.6 92.5 %copy-start.3 = (s32[16]{0:T(128)S(1)}, s32[16]{0:T(128)}, u32[]{:S(2)}) copy-start(s32[16]{0:T(128)} %param.10) | copy-start | bytes 196
  0.6 92.5 %copy-start = (bf16[2,4096]{1,0:T(2,128)(2,1)S(1)}, bf16[2,4096]{1,0:T(2,128)(2,1)}, u32[]{:S(2)}) copy-start(bf16[2,4096]{1,0:T(2,128)(2,1)} %param.8) | copy-start | bytes 49156
  76.0 39.4 %all-to-all-start = ((s32[128,1,4]{2,1,0:T(1,128)}), s32[128,1,4]{2,1,0:T(1,128)S(1)}, u32[]{:S(2)}, u32[]{:S(2)}) async-start(s32[128,1,4]{2,1,0:T(1,128)} %bitcast.8), calls=%async_computation | async-start | bytes 131072 | tf_op jit(solution)/shard_map/all_to_all | solution.py:34
  119.8 23.2 %all-to-all-start.1 = ((bf16[128,4,2,256]{3,2,1,0:T(2,128)(2,1)}), bf16[128,4,2,256]{3,2,1,0:T(2,128)(2,1)S(1)}, u32[]{:S(2)}, u32[]{:S(2)}) async-start(bf16[128,4,2,256]{3,2,1,0:T(2,128)(2,1)} %broadcast_multiply_fusion.1), calls=%async_computation.1 | async-start | bytes 1048576 | tf_op jit(solution)/shard_map/all_to_all | solution.py:54
  143.0 23.5 %all-to-all-start.2 = ((f32[128,4,2,256]{3,1,2,0:T(4,128)}), f32[128,4,2,256]{3,1,2,0:T(4,128)S(1)}, u32[]{:S(2)}, u32[]{:S(2)}) async-start(f32[128,4,2,256]{3,1,2,0:T(4,128)} %copy.88), calls=%async_computation.2 | async-start | bytes 2097152 | tf_op jit(solution)/shard_map/all_to_all | solution.py:89
  157.3 10.1 %copy-start.2 = (f32[2,4096]{1,0:T(2,128)S(1)}, f32[2,4096]{1,0:T(2,128)}, u32[]{:S(2)}) copy-start(f32[2,4096]{1,0:T(2,128)} %param.9) | copy-start | bytes 98308
  167.5 10.5 %copy-start.1 = (f32[1,2,16,256]{3,1,2,0:T(2,128)}, f32[1,2,16,256]{3,1,2,0:T(2,128)S(1)}, u32[]{:S(2)}) copy-start(f32[1,2,16,256]{3,1,2,0:T(2,128)S(1)} %copy.98) | copy-start | bytes 98308
  179.4 24.1 %all-to-all-start.3 = ((bf16[128,4,2,256]{3,2,1,0:T(2,128)(2,1)}), bf16[128,4,2,256]{3,2,1,0:T(2,128)(2,1)S(1)}, u32[]{:S(2)}, u32[]{:S(2)}) async-start(bf16[128,4,2,256]{3,2,1,0:T(2,128)(2,1)} %broadcast_multiply_fusion), calls=%async_computation.3 | async-start | bytes 1048576 | tf_op jit(solution)/shard_map/all_to_all | solution.py:54
  203.5 28.6 %all-to-all-start.4 = ((f32[128,4,2,256]{3,1,2,0:T(4,128)}), f32[128,4,2,256]{3,1,2,0:T(4,128)S(1)}, u32[]{:S(2)}, u32[]{:S(2)}) async-start(f32[128,4,2,256]{3,1,2,0:T(4,128)} %copy.96), calls=%async_computation.4 | async-start | bytes 2097152 | tf_op jit(solution)/shard_map/all_to_all | solution.py:89
where the time goes:
time: 234 us
  blocking collectives  68.7 us (29%)
  local copies, waits for them, and re-layouts  57.3 us (24%)
  matrix products  43.2 us (18%)
  starting transfers between devices  33.9 us (14%)
  waiting for transfers between devices  23.2 us (10%)
  other arithmetic  6.33 us (3%)
    unnamed x1, blocking collectives  68.7 us
    scatter x2, local copies, waits for them, and re-layouts, apply_kernel(): outgoing = jnp.zeros((devices * capacity, 2, block_size), jnp.float32).at...  24 us
    all_to_all x2, waiting for transfers between devices, apply_kernel(): lax.all_to_all(outgoing, ('wide', 'narrow'), split_axis=0, concat_axis=0,...  16.9 us
    all_to_all x2, starting transfers between devices, apply_kernel(): lax.all_to_all(reply_blocks, ('wide', 'narrow'), split_axis=0, concat_axi...  14.7 us
    all_to_all x2, starting transfers between devices, apply_kernel(): lax.all_to_all(outgoing, ('wide', 'narrow'), split_axis=0, concat_axis=0,...  14.6 us
    dot_general x2, matrix products, apply_kernel(): jnp.einsum('erb,ecr->ecb', v_factor, projected, preferred_element_type=jn...  14.3 us
    dot_general x2, matrix products, apply_kernel(): jnp.einsum('erb,ecr->ecb', u_factor, reduced, preferred_element_type=jnp....  14.3 us
    dot_general x2, matrix products, apply_kernel(): jnp.einsum('nij,ncj->nci', near_block, near_rates, preferred_element_type...  11.3 us
  transfers between devices with their start and end apart: 5, of which 3 were waited for; matrix products, arithmetic and copies ran while one was open for 35% of the time, Pallas kernels for 0%

commit v1 on v0

v1 whole, which is shorter than its diff:
```python
import functools

import jax
import jax.numpy as jnp
from jax import lax
from jax.experimental import pallas as pl
from jax.experimental.pallas import tpu as pltpu
from jax.sharding import PartitionSpec as P

AXES = ("wide", "narrow")
MESH = pl.DeviceIdType.MESH
BF = jnp.bfloat16
F32 = jnp.float32
I32 = jnp.int32
STRIDE = 37


def dot_nt(a, b):
    return lax.dot_general(a, b, (((1,), (1,)), ((), ())), preferred_element_type=F32)


def dot_nn(a, b):
    return lax.dot_general(a, b, (((1,), (0,)), ((), ())), preferred_element_type=F32)


def hot(mask):
    return jnp.where(mask, 1.0, 0.0).astype(BF)


def iota(shape, dim):
    return lax.broadcasted_iota(I32, shape, dim)


def rows_at(start, size):
    return pl.ds(pl.multiple_of(start, size), size)


def kernel(
    dims,
    home, far, near_list, x_in, effect, u_hbm, v_hbm, near_hbm,
    first_out, second_out,
    u, v, near, index, pair_hot, slot_val, order, tri, slot_hot, row_sel, row_sel_t,
    near_place, near_cols, near_left, col_sel, col_sel_t, reply_sel, reply_sel_t, rep,
    left, mid, terms, terms_low, flat,
    sent, got,
    load_sem, gather_send, gather_recv, send_sem, recv_sem,
):
    wide_n, narrow_n, nb, cap, adm, near_n, block, rank = dims
    devices = wide_n * narrow_n
    tiles = adm // 8
    cols2 = 2 * adm
    per = 2 * cap
    index_rows = index.shape[1] - 1
    half = block // 2
    my_wide = lax.axis_index("wide")
    my_narrow = lax.axis_index("narrow")
    me = my_wide * narrow_n + my_narrow

    loads = [
        pltpu.make_async_copy(u_hbm, u, load_sem.at[0]),
        pltpu.make_async_copy(v_hbm, v, load_sem.at[1]),
        pltpu.make_async_copy(near_hbm, near, load_sem.at[2]),
    ]
    for load in loads:
        load.start()

    def narrow_peer(j):
        return (my_wide, lax.rem(my_narrow + j, narrow_n))

    def wide_peer(j):
        return (lax.rem(my_wide + j, wide_n), my_narrow)

    barrier = pltpu.get_barrier_semaphore()
    for j in range(1, narrow_n):
        pl.semaphore_signal(barrier, inc=1, device_id=narrow_peer(j), device_id_type=MESH)
    for j in range(1, wide_n):
        pl.semaphore_signal(barrier, inc=1, device_id=wide_peer(j), device_id_type=MESH)

    far_cols = far[1:2, :]
    for r in range(index_rows):
        width = min(128, adm - r * 128)
        piece = far_cols[:, r * 128 : r * 128 + width]
        if width < 128:
            piece = jnp.concatenate([piece, jnp.full((1, 128 - width), -1, I32)], axis=1)
        index[me, r : r + 1, :] = piece
    lane = iota((1, 128), 1)
    home_row = jnp.full((1, 128), -1, I32)
    for s in range(nb):
        home_row = jnp.where(lane == s, home[s], home_row)
    index[me, index_rows : index_rows + 1, :] = home_row

    pl.semaphore_wait(barrier, narrow_n + wide_n - 2)

    for j in range(1, narrow_n):
        pltpu.make_async_remote_copy(
            src_ref=index.at[me], dst_ref=index.at[me],
            send_sem=gather_send.at[0], recv_sem=gather_recv.at[0],
            device_id=narrow_peer(j), device_id_type=MESH,
        ).start()

    row_slot = jnp.zeros((1, adm), I32)
    near_row = jnp.zeros((1, near_n), I32)
    near_col = jnp.zeros((1, near_n), I32)
    far_rows = far[0:1, :]
    for s in range(nb):
        row_slot = jnp.where(far_rows == home[s], s, row_slot)
        near_row = jnp.where(near_list[0:1, :] == home[s], s, near_row)
        near_col = jnp.where(near_list[1:2, :] == home[s], s, near_col)
    place = iota((cols2, adm), 0)
    slot_hot[...] = hot(lax.div(place, 16) * 8 + lax.rem(place, 8) == far[2:3, :])
    row_hot = hot(row_slot == lax.rem(iota((2 * nb, adm), 0), nb))
    pick = dot_nt(slot_hot[...], row_hot)
    comp = lax.rem(lax.div(iota((cols2, 2 * nb), 0), 8), 2)
    row_sel[...] = jnp.where(comp == lax.div(iota((cols2, 2 * nb), 1), nb), pick, 0.0).astype(BF)
    pick_t = dot_nt(row_hot, slot_hot[...])
    comp_t = lax.rem(lax.div(iota((2 * nb, cols2), 1), 8), 2)
    row_sel_t[...] = jnp.where(comp_t == lax.div(iota((2 * nb, cols2), 0), nb), pick_t, 0.0).astype(BF)
    tri[...] = hot(iota((adm, adm), 0) < iota((adm, adm), 1))

    near_key = near_list[2:3, :] * nb + near_row
    near_key2 = jnp.concatenate([near_key, near_key], axis=1)
    near_col2 = jnp.concatenate([near_col, near_col], axis=1)
    near_rows = near_n * 2 * nb
    where_row = iota((near_rows, 2 * near_n), 0)
    row_key = lax.div(where_row, 2 * nb) * nb + lax.rem(where_row, nb)
    row_comp = lax.rem(lax.div(where_row, nb), 2)
    lane_comp = lax.div(iota((near_rows, 2 * near_n), 1), near_n)
    near_place[...] = hot((row_key == near_key2) & (row_comp == lane_comp))
    col_row = iota((2 * nb, 2 * near_n), 0)
    col_mask = (near_col2 == lax.rem(col_row, nb)) & (
        lax.div(col_row, nb) == lax.div(iota((2 * nb, 2 * near_n), 1), near_n)
    )
    near_cols[...] = jnp.where(col_mask, 1.0, 0.0).T.astype(BF)

    chunk = 2 * per
    rep_rows = devices * per
    rep[...] = hot(lax.div(iota((rep_rows, devices), 0), per) == iota((rep_rows, devices), 1))

    def wait_bytes(ref, sem):
        pltpu.make_async_copy(ref, ref, sem).wait()

    wait_bytes(index.at[pl.ds(0, narrow_n - 1)], gather_recv.at[0])
    row_group = index.at[pl.ds(my_wide * narrow_n, narrow_n)]
    for j in range(1, wide_n):
        pltpu.make_async_remote_copy(
            src_ref=row_group, dst_ref=row_group,
            send_sem=gather_send.at[1], recv_sem=gather_recv.at[1],
            device_id=wide_peer(j), device_id_type=MESH,
        ).start()

    diag = lax.rem(iota((16, 8 * rank), 0), 8) == lax.div(iota((16, 8 * rank), 1), rank)
    unroll = 8 if tiles % 8 == 0 else 1

    def over_tiles(step):
        def body(i, carry):
            for k in range(unroll):
                step(i * unroll + k)
            return carry

        lax.fori_loop(0, tiles // unroll, body, 0)

    def contract(factor):
        def step(t):
            y = dot_nt(left[rows_at(t * 16, 16), :], factor[rows_at(t * 8 * rank, 8 * rank), :])
            mid[rows_at(t * 16, 16), :] = jnp.where(diag, y, 0.0).astype(BF)

        over_tiles(step)

    def expand(factor, split):
        def step(t):
            y = dot_nn(mid[rows_at(t * 16, 16), :], factor[rows_at(t * 8 * rank, 8 * rank), :])
            high = y.astype(BF)
            terms[rows_at(t * 16, 16), :] = high
            if split:
                terms_low[rows_at(t * 16, 16), :] = (y - high.astype(F32)).astype(BF)

        over_tiles(step)

    def send_all(n):
        def body(j, carry):
            to = lax.rem(me + j * STRIDE, devices)
            pltpu.make_async_remote_copy(
                src_ref=sent.at[n, to], dst_ref=got.at[n, me],
                send_sem=send_sem.at[n], recv_sem=recv_sem.at[n],
                device_id=(lax.div(to, narrow_n), lax.rem(to, narrow_n)), device_id_type=MESH,
            ).start()
            return carry

        lax.fori_loop(1, devices, body, 0)
        got[n, me] = sent[n, me]

    def stage(n, sel, right):
        parts = max(1, rep_rows // 256)
        size = rep_rows // parts

        def body(i, carry):
            y = dot_nn(sel[rows_at(i * size, size), :], right)
            y = y.reshape(size // per, per, block)
            y = jnp.concatenate([y[:, :, :half], y[:, :, half:]], axis=1)
            sent[n, rows_at(i * (size // per), size // per)] = y.astype(BF)
            return carry

        lax.fori_loop(0, parts, body, 0)

    def land(n):
        wait_bytes(got.at[n, pl.ds(0, devices - 1)], recv_sem.at[n])
        y = got[n].astype(F32)
        y = jnp.concatenate([y[:, :per, :], y[:, per:, :]], axis=2)
        flat[...] = y.reshape(rep_rows, block).astype(BF)

    def send_rates(n, x):
        stage(n, reply_sel, jnp.concatenate([x] * cap, axis=0))
        send_all(n)

    def near_part(x):
        near_x = dot_nn(near_cols[...], x).astype(BF)
        parts = max(1, near_rows // 256)
        size = near_rows // parts

        def place_body(i, carry):
            near_left[rows_at(i * size, size), :] = dot_nn(
                near_place[rows_at(i * size, size), :], near_x
            ).astype(BF)
            return carry

        lax.fori_loop(0, parts, place_body, 0)
        steps = 4

        def body(i, acc):
            for k in range(steps):
                g = i * steps + k
                acc = acc + dot_nt(
                    near_left[rows_at(g * 2 * nb, 2 * nb), :], near[rows_at(g * block, block), :]
                )
            return acc

        return lax.fori_loop(0, near_n // steps, body, jnp.zeros((2 * nb, block), F32))

    def row_rates(x):
        left[...] = dot_nn(row_sel[...], x).astype(BF)

    def send_back(n):
        stage(n, col_sel_t, terms[...])
        send_all(n)

    def finish(n_rates, n_back, total):
        land(n_rates)
        left[...] = dot_nn(col_sel[...], flat[...]).astype(BF)
        contract(v)
        expand(u, True)
        total = total + dot_nn(row_sel_t[...], terms[...])
        total = total + dot_nn(row_sel_t[...], terms_low[...])
        land(n_back)
        return total + dot_nn(reply_sel_t[...], flat[...])

    x = x_in[...]
    row_rates(x)
    loads[0].wait()
    contract(u)

    wait_bytes(index.at[pl.ds(0, (wide_n - 1) * narrow_n)], gather_recv.at[1])
    part = min(32, devices)
    for q in range(0, devices, part):
        wanted = jnp.concatenate(
            [index[q : q + part, r, :] for r in range(index_rows)], axis=1
        )[:, :adm]
        val = jnp.zeros((part, adm), F32)
        homes = index[q : q + part, index_rows, :]
        found = jnp.zeros((part, adm), F32)
        for s in range(nb):
            val = jnp.where(wanted == home[s], float(s + 1), val)
            found = jnp.where(homes[:, s : s + 1] == far_cols, 1.0, found)
        slot_val[q : q + part, :] = val
        pair_hot[q : q + part, :] = hot(val > 0.0)
        pair_hot[devices + q : devices + q + part, :] = found.astype(BF)
    order[...] = dot_nn(pair_hot[...], tri[...])
    lane_k = lax.div(iota((devices, 2 * nb * cap), 1), 2 * nb)
    lane_s = lax.rem(iota((devices, 2 * nb * cap), 1), nb) + 1
    chosen = jnp.zeros((devices, 2 * nb * cap), F32)
    for k in range(cap):
        slot_k = jnp.sum(
            jnp.where(order[:devices, :] == float(k), slot_val[...], 0.0), axis=1, keepdims=True
        )
        chosen = jnp.where(lane_k == k, slot_k, chosen)
    asked = jnp.where(chosen == lane_s.astype(F32), 1.0, 0.0)
    lanes = 2 * nb * cap
    reply_row = lax.rem(iota((rep_rows, lanes), 0), per)
    reply_mask = reply_row == lax.div(iota((rep_rows, lanes), 1), nb)
    reply_sel[...] = jnp.where(reply_mask, dot_nn(rep[...], asked.astype(BF)), 0.0).astype(BF)
    send_rates(0, x)

    reply_col = lax.rem(iota((lanes, rep_rows), 1), per)
    back_mask = reply_col == lax.div(iota((lanes, rep_rows), 0), nb)
    back_sel = jnp.where(back_mask, dot_nt(asked.T.astype(BF), rep[...]), 0.0)
    summed = back_sel[: 2 * nb]
    for k in range(1, cap):
        summed = summed + back_sel[2 * nb * k : 2 * nb * (k + 1)]
    reply_sel_t[...] = summed.astype(BF)

    found = pair_hot[devices:, :].astype(F32)
    owner = jnp.sum(found * iota((devices, adm), 0).astype(F32), axis=0, keepdims=True)
    place_in = jnp.sum(found * order[devices:, :], axis=0, keepdims=True)
    both = jnp.concatenate([owner, place_in, jnp.zeros((6, adm), F32)], axis=0).astype(BF)
    to_row = dot_nt(both, slot_hot[...])
    to_row = (to_row[0:1] * per + to_row[1:2] * 2).astype(I32)
    to_row = to_row + lax.rem(lax.div(iota((1, cols2), 1), 8), 2)
    col_sel_t[...] = hot(iota((rep_rows, cols2), 0) == to_row)
    to_col = dot_nt(slot_hot[...], both)
    to_col = (to_col[:, 0:1] * per + to_col[:, 1:2] * 2).astype(I32)
    to_col = to_col + lax.rem(lax.div(iota((cols2, 1), 0), 8), 2)
    col_sel[...] = hot(iota((cols2, rep_rows), 1) == to_col)

    loads[1].wait()
    expand(v, False)
    send_back(1)
    loads[2].wait()
    first = finish(0, 1, near_part(x))
    first_out[...] = first

    x = (x.astype(F32) * jnp.exp(jnp.tanh(first / effect[...]))).astype(BF)
    send_rates(2, x)
    row_rates(x)
    contract(u)
    expand(v, False)
    send_back(3)
    second_out[...] = finish(2, 3, near_part(x))

    wait_bytes(index.at[pl.ds(0, narrow_n - 1)], gather_send.at[0])
    wait_bytes(index.at[pl.ds(0, (wide_n - 1) * narrow_n)], gather_send.at[1])
    for n in range(4):
        wait_bytes(sent.at[n, pl.ds(0, devices - 1)], send_sem.at[n])


def local(slip, effect_stress, home_blocks, far_list, u_factor, v_factor, near_list, near_block):
    wide_n, narrow_n = lax.axis_size("wide"), lax.axis_size("narrow")
    devices = wide_n * narrow_n
    nb = home_blocks.shape[0]
    block = slip.shape[1] // nb
    adm, rank, _ = u_factor.shape
    near_n = near_list.shape[1]
    cap = max(2, adm // devices + 1)
    per = 2 * cap
    rep_rows = devices * per
    cols2 = 2 * adm
    index_rows = -(-adm // 128)
    dims = (wide_n, narrow_n, nb, cap, adm, near_n, block, rank)
    vmem = pl.BlockSpec(memory_space=pltpu.VMEM)
    smem = pl.BlockSpec(memory_space=pltpu.SMEM)
    hbm = pl.BlockSpec(memory_space=pl.ANY)
    field = jax.ShapeDtypeStruct((2 * nb, block), F32)
    dma = pltpu.SemaphoreType.DMA
    first, second = pl.pallas_call(
        functools.partial(kernel, dims),
        out_shape=(field, field),
        in_specs=[smem, vmem, vmem, vmem, vmem, hbm, hbm, hbm],
        out_specs=(vmem, vmem),
        scratch_shapes=[
            pltpu.VMEM((adm * rank, block), BF),
            pltpu.VMEM((adm * rank, block), BF),
            pltpu.VMEM((near_n * block, block), BF),
            pltpu.VMEM((devices, index_rows + 1, 128), I32),
            pltpu.VMEM((2 * devices, adm), BF),
            pltpu.VMEM((devices, adm), F32),
            pltpu.VMEM((2 * devices, adm), F32),
            pltpu.VMEM((adm, adm), BF),
            pltpu.VMEM((cols2, adm), BF),
            pltpu.VMEM((cols2, 2 * nb), BF),
            pltpu.VMEM((2 * nb, cols2), BF),
            pltpu.VMEM((near_n * 2 * nb, 2 * near_n), BF),
            pltpu.VMEM((2 * near_n, 2 * nb), BF),
            pltpu.VMEM((near_n * 2 * nb, block), BF),
            pltpu.VMEM((cols2, rep_rows), BF),
            pltpu.VMEM((rep_rows, cols2), BF),
            pltpu.VMEM((rep_rows, 2 * nb * cap), BF),
            pltpu.VMEM((2 * nb, rep_rows), BF),
            pltpu.VMEM((rep_rows, devices), BF),
            pltpu.VMEM((cols2, block), BF),
            pltpu.VMEM((cols2, 8 * rank), BF),
            pltpu.VMEM((cols2, block), BF),
            pltpu.VMEM((cols2, block), BF),
            pltpu.VMEM((rep_rows, block), BF),
            pltpu.VMEM((4, devices, 2 * per, block // 2), BF),
            pltpu.VMEM((4, devices, 2 * per, block // 2), BF),
            dma((3,)),
            dma((2,)),
            dma((2,)),
            dma((4,)),
            dma((4,)),
        ],
        compiler_params=pltpu.CompilerParams(
            collective_id=0, has_side_effects=True, vmem_limit_bytes=56 << 20
        ),
        name="stress_two_steps",
    )(
        home_blocks,
        far_list,
        near_list,
        slip.reshape(2 * nb, block),
        effect_stress.reshape(2 * nb, block),
        u_factor.reshape(adm * rank, block),
        v_factor.reshape(adm * rank, block),
        near_block.reshape(near_n * block, block),
    )
    return first.reshape(2, nb * block), second.reshape(2, nb * block)


def solution(mesh):
    in_specs = (
        P(None, AXES),
        P(None, AXES),
        P(AXES),
        P(None, AXES),
        P(AXES, None, None),
        P(AXES, None, None),
        P(None, AXES),
        P(AXES, None, None),
    )
    out_specs = (P(None, AXES), P(None, AXES))
    return jax.shard_map(local, mesh=mesh, in_specs=in_specs, out_specs=out_specs, check_vma=False)
```

time: 234 us -> 69 us (0.29)
  blocking collectives: 68.7 us -> 0 us
  Pallas kernels: 0 us -> 62.4 us
  local copies, waits for them, and re-layouts: 57.3 us -> 5.53 us
  matrix products: 43.2 us -> 0 us
  starting transfers between devices: 33.9 us -> 0 us
  waiting for transfers between devices: 23.2 us -> 0 us
  other arithmetic: 6.33 us -> 0 us
    unnamed x1 -> x0, blocking collectives: 68.7 us -> none
    pallas_call x0 -> x1, Pallas kernels: none -> 62.4 us  [local(): pl.pallas_call(functools.partial(kernel, dims), out_shape=(field, field),...]
    dot_general x16 -> x0, matrix products: 43.2 us -> none  [the longest x2 14.3 us: apply_kernel(): jnp.einsum('erb,ecr->ecb', v_factor, projected, preferred_element_type=jn...]
    all_to_all x5 -> x0, starting transfers between devices: 33.9 us -> none  [the longest x2 14.7 us: apply_kernel(): lax.all_to_all(reply_blocks, ('wide', 'narrow'), split_axis=0, concat_axi...]
    scatter x5 -> x0, local copies, waits for them, and re-layouts: 30.8 us -> none  [the longest x2 24 us: apply_kernel(): outgoing = jnp.zeros((devices * capacity, 2, block_size), jnp.float32).at...]
    all_to_all x5 -> x0, waiting for transfers between devices: 23.2 us -> none  [the longest x2 16.9 us: apply_kernel(): lax.all_to_all(outgoing, ('wide', 'narrow'), split_axis=0, concat_axis=0,...]
    gather x8 -> x0, local copies, waits for them, and re-layouts: 17.3 us -> none  [the longest x2 5.14 us: apply_kernel(): reply_blocks = xblocks[wanted] * incoming_valid]
    mul x2 -> x0, other arithmetic: 2.86 us -> none  [apply_kernel(): reply_blocks = xblocks[wanted] * incoming_valid]
  transfers between devices with their start and end apart: 5 -> 0, of which waited for: 3 -> 0; matrix products, arithmetic and copies ran while one was open for 35% -> 0% of each run, Pallas kernels for 0% -> 0%
where the time goes in v1:
time: 69 us; the launch traced here: 68.6 us
  Pallas kernels  62.4 us (90%)
  local copies, waits for them, and re-layouts  5.53 us (8%)
    pallas_call x1, Pallas kernels, local(): pl.pallas_call(functools.partial(kernel, dims), out_shape=(field, field),...  62.4 us
    reshape x2, local copies, waits for them, and re-layouts, local(): return (first.reshape(2, nb * block), second.reshape(2, nb * block))  2.79 us
    reshape x1, local copies, waits for them, and re-layouts, local(): effect_stress.reshape(2 * nb, block)  1.4 us

profile of v1, /device:TPU:1, one launch (start us, length us, event | category | flops | bytes accessed | tf_op | source)
XLA Modules:
  0.0 68.6 jit_solution(8538595611222248459)
XLA Ops:
  0.6 1.3 %reshape.25.x_in = bf16[32,256]{1,0:T(8,128)(2,1)} reshape(bf16[2,4096]{1,0:T(2,128)(2,1)} %param.8) | data formatting | bytes 32768 | tf_op jit(solution)/shard_map/reshape | solution.py:398
  2.0 1.4 %reshape.26.effect = f32[32,256]{1,0:T(8,128)} reshape(f32[2,4096]{1,0:T(2,128)} %param.9) | data formatting | bytes 65536 | tf_op jit(solution)/shard_map/reshape | solution.py:399
  3.4 62.4 %stress_two_steps.1 = (f32[32,256]{1,0:T(8,128)}, f32[32,256]{1,0:T(8,128)}) custom-call(s32[16]{0:T(128)} %home.1, s32[3,384]{1,0:T(4,128)} %far.1, s32[3,64]{1,0:T(4,128)} %near_list.1, bf16[32,256]{1,0:T(8,128)(2,1)} %reshape.25.x_in, f32[32,256]{1,0:T(8,128)} %reshape.26.effect, bf16[12288,256]{1,0:T(8,128)(2,1)} %bitcast.4, bf16[12288,256]{1,0:T(8,128)(2,1)} %bitcast.5, ...), custom_call_target="tpu_custom_call" | custom-call | tf_op jit(solution)/shard_map/stress_two_steps/pallas_call | solution.py:352
  65.8 1.4 %reshape.30 = f32[2,4096]{1,0:T(2,128)} reshape(f32[32,256]{1,0:T(8,128)} %get-tuple-element.4) | data formatting | bytes 65536 | tf_op jit(solution)/shard_map/reshape | solution.py:404
  67.2 1.4 %reshape.31 = f32[2,4096]{1,0:T(2,128)} reshape(f32[32,256]{1,0:T(8,128)} %get-tuple-element.5) | data formatting | bytes 65536 | tf_op jit(solution)/shard_map/reshape | solution.py:404

commit v2 on v1

--- a/solution.py
+++ b/solution.py
@@ -1,4 +1,5 @@
 import functools
+import itertools
 
 import jax
 import jax.numpy as jnp
@@ -12,7 +13,6 @@
 BF = jnp.bfloat16
 F32 = jnp.float32
 I32 = jnp.int32
-STRIDE = 37
 
 
 def dot_nt(a, b):
@@ -31,18 +31,26 @@
     return lax.broadcasted_iota(I32, shape, dim)
 
 
+def far_first(extents):
+    def hops(shift):
+        return sum(min(d, n - d) for d, n, core in zip(shift, extents, (0, 1, 0, 0)) if not core)
+
+    shifts = [s for s in itertools.product(*map(range, extents)) if any(s)]
+    return sorted(shifts, key=hops, reverse=True)
+
+
 def rows_at(start, size):
     return pl.ds(pl.multiple_of(start, size), size)
 
 
 def kernel(
     dims,
-    home, far, near_list, x_in, effect, u_hbm, v_hbm, near_hbm,
+    home, far, near_list, slip, effect, u_hbm, v_hbm, near_hbm,
     first_out, second_out,
     u, v, near, index, pair_hot, slot_val, order, tri, slot_hot, row_sel, row_sel_t,
     near_place, near_cols, near_left, col_sel, col_sel_t, reply_sel, reply_sel_t, rep,
     left, mid, terms, terms_low, flat,
-    sent, got,
+    sent, got, field,
     load_sem, gather_send, gather_recv, send_sem, recv_sem,
 ):
     wide_n, narrow_n, nb, cap, adm, near_n, block, rank = dims
@@ -136,6 +144,19 @@
     rep_rows = devices * per
     rep[...] = hot(lax.div(iota((rep_rows, devices), 0), per) == iota((rep_rows, devices), 1))
 
+    def by_block(ref):
+        for c in range(2):
+            for s in range(nb):
+                piece = ref[c : c + 1, s * block : (s + 1) * block]
+                field[c * nb + s : c * nb + s + 1, :] = piece.astype(F32)
+        return field[...]
+
+    def by_patch(value, ref):
+        field[...] = value
+        for c in range(2):
+            for s in range(nb):
+                ref[c : c + 1, s * block : (s + 1) * block] = field[c * nb + s : c * nb + s + 1, :]
+
     def wait_bytes(ref, sem):
         pltpu.make_async_copy(ref, ref, sem).wait()
 
@@ -176,17 +197,30 @@
 
         over_tiles(step)
 
+    wide_y, wide_c = wide_n // 2, 2
+    narrow_x = 4 if narrow_n % 4 == 0 and narrow_n > 4 else 2
+    narrow_z = narrow_n // narrow_x
+    extents = (wide_y, wide_c, narrow_x, narrow_z)
+    shifted_wide = {
+        (dy, dc): lax.rem(my_wide // wide_c + dy, wide_y) * wide_c + lax.rem(my_wide % wide_c + dc, wide_c)
+        for dy in range(wide_y)
+        for dc in range(wide_c)
+    }
+    shifted_narrow = {
+        (dx, dz): lax.rem(my_narrow // narrow_z + dx, narrow_x) * narrow_z
+        + lax.rem(my_narrow % narrow_z + dz, narrow_z)
+        for dx in range(narrow_x)
+        for dz in range(narrow_z)
+    }
+
     def send_all(n):
-        def body(j, carry):
-            to = lax.rem(me + j * STRIDE, devices)
+        for dy, dc, dx, dz in far_first(extents):
+            to_wide, to_narrow = shifted_wide[dy, dc], shifted_narrow[dx, dz]
             pltpu.make_async_remote_copy(
-                src_ref=sent.at[n, to], dst_ref=got.at[n, me],
+                src_ref=sent.at[n, to_wide * narrow_n + to_narrow], dst_ref=got.at[n, me],
                 send_sem=send_sem.at[n], recv_sem=recv_sem.at[n],
-                device_id=(lax.div(to, narrow_n), lax.rem(to, narrow_n)), device_id_type=MESH,
+                device_id=(to_wide, to_narrow), device_id_type=MESH,
             ).start()
-            return carry
-
-        lax.fori_loop(1, devices, body, 0)
         got[n, me] = sent[n, me]
 
     def stage(n, sel, right):
@@ -253,7 +287,7 @@
         land(n_back)
         return total + dot_nn(reply_sel_t[...], flat[...])
 
-    x = x_in[...]
+    x = by_block(slip).astype(BF)
     row_rates(x)
     loads[0].wait()
     contract(u)
@@ -265,21 +299,17 @@
             [index[q : q + part, r, :] for r in range(index_rows)], axis=1
         )[:, :adm]
         val = jnp.zeros((part, adm), F32)
-        homes = index[q : q + part, index_rows, :]
-        found = jnp.zeros((part, adm), F32)
         for s in range(nb):
             val = jnp.where(wanted == home[s], float(s + 1), val)
-            found = jnp.where(homes[:, s : s + 1] == far_cols, 1.0, found)
         slot_val[q : q + part, :] = val
         pair_hot[q : q + part, :] = hot(val > 0.0)
-        pair_hot[devices + q : devices + q + part, :] = found.astype(BF)
     order[...] = dot_nn(pair_hot[...], tri[...])
     lane_k = lax.div(iota((devices, 2 * nb * cap), 1), 2 * nb)
     lane_s = lax.rem(iota((devices, 2 * nb * cap), 1), nb) + 1
     chosen = jnp.zeros((devices, 2 * nb * cap), F32)
     for k in range(cap):
         slot_k = jnp.sum(
-            jnp.where(order[:devices, :] == float(k), slot_val[...], 0.0), axis=1, keepdims=True
+            jnp.where(order[...] == float(k), slot_val[...], 0.0), axis=1, keepdims=True
         )
         chosen = jnp.where(lane_k == k, slot_k, chosen)
     asked = jnp.where(chosen == lane_s.astype(F32), 1.0, 0.0)
@@ -297,9 +327,17 @@
         summed = summed + back_sel[2 * nb * k : 2 * nb * (k + 1)]
     reply_sel_t[...] = summed.astype(BF)
 
-    found = pair_hot[devices:, :].astype(F32)
+    for q in range(0, devices, part):
+        homes = index[q : q + part, index_rows, :]
+        found = jnp.zeros((part, adm), F32)
+        for s in range(nb):
+            found = jnp.where(homes[:, s : s + 1] == far_cols, 1.0, found)
+        slot_val[q : q + part, :] = found
+        pair_hot[q : q + part, :] = found.astype(BF)
+    order[...] = dot_nn(pair_hot[...], tri[...])
+    found = slot_val[...]
     owner = jnp.sum(found * iota((devices, adm), 0).astype(F32), axis=0, keepdims=True)
-    place_in = jnp.sum(found * order[devices:, :], axis=0, keepdims=True)
+    place_in = jnp.sum(found * order[...], axis=0, keepdims=True)
     both = jnp.concatenate([owner, place_in, jnp.zeros((6, adm), F32)], axis=0).astype(BF)
     to_row = dot_nt(both, slot_hot[...])
     to_row = (to_row[0:1] * per + to_row[1:2] * 2).astype(I32)
@@ -315,15 +353,15 @@
     send_back(1)
     loads[2].wait()
     first = finish(0, 1, near_part(x))
-    first_out[...] = first
-
-    x = (x.astype(F32) * jnp.exp(jnp.tanh(first / effect[...]))).astype(BF)
+    by_patch(first, first_out)
+
+    x = (x.astype(F32) * jnp.exp(jnp.tanh(first / by_block(effect)))).astype(BF)
     send_rates(2, x)
     row_rates(x)
     contract(u)
     expand(v, False)
     send_back(3)
-    second_out[...] = finish(2, 3, near_part(x))
+    by_patch(finish(2, 3, near_part(x)), second_out)
 
     wait_bytes(index.at[pl.ds(0, narrow_n - 1)], gather_send.at[0])
     wait_bytes(index.at[pl.ds(0, (wide_n - 1) * narrow_n)], gather_send.at[1])
@@ -347,9 +385,9 @@
     vmem = pl.BlockSpec(memory_space=pltpu.VMEM)
     smem = pl.BlockSpec(memory_space=pltpu.SMEM)
     hbm = pl.BlockSpec(memory_space=pl.ANY)
-    field = jax.ShapeDtypeStruct((2 * nb, block), F32)
+    field = jax.ShapeDtypeStruct((2, nb * block), F32)
     dma = pltpu.SemaphoreType.DMA
-    first, second = pl.pallas_call(
+    return pl.pallas_call(
         functools.partial(kernel, dims),
         out_shape=(field, field),
         in_specs=[smem, vmem, vmem, vmem, vmem, hbm, hbm, hbm],
@@ -359,9 +397,9 @@
             pltpu.VMEM((adm * rank, block), BF),
             pltpu.VMEM((near_n * block, block), BF),
             pltpu.VMEM((devices, index_rows + 1, 128), I32),
-            pltpu.VMEM((2 * devices, adm), BF),
+            pltpu.VMEM((devices, adm), BF),
             pltpu.VMEM((devices, adm), F32),
-            pltpu.VMEM((2 * devices, adm), F32),
+            pltpu.VMEM((devices, adm), F32),
             pltpu.VMEM((adm, adm), BF),
             pltpu.VMEM((cols2, adm), BF),
             pltpu.VMEM((cols2, 2 * nb), BF),
@@ -381,6 +419,7 @@
             pltpu.VMEM((rep_rows, block), BF),
             pltpu.VMEM((4, devices, 2 * per, block // 2), BF),
             pltpu.VMEM((4, devices, 2 * per, block // 2), BF),
+            pltpu.VMEM((2 * nb, block), F32),
             dma((3,)),
             dma((2,)),
             dma((2,)),
@@ -395,13 +434,12 @@
         home_blocks,
         far_list,
         near_list,
-        slip.reshape(2 * nb, block),
-        effect_stress.reshape(2 * nb, block),
+        slip,
+        effect_stress,
         u_factor.reshape(adm * rank, block),
         v_factor.reshape(adm * rank, block),
         near_block.reshape(near_n * block, block),
     )
-    return first.reshape(2, nb * block), second.reshape(2, nb * block)
 
 
 def solution(mesh):

time: 69 us -> 62.1 us (0.900)
  Pallas kernels: 62.4 us -> 58.4 us
  local copies, waits for them, and re-layouts: 5.53 us -> 2.75 us
    reshape x4 -> x0, local copies, waits for them, and re-layouts: 5.53 us -> none  [the longest x2 2.79 us: local(): return (first.reshape(2, nb * block), second.reshape(2, nb * block))]
    pallas_call x1, Pallas kernels: 62.4 us -> 58.4 us  [local(): pl.pallas_call(functools.partial(kernel, dims), out_shape=(field, field),...]
    unnamed x0 -> x2, local copies, waits for them, and re-layouts: none -> 2.75 us
where the time goes in v2:
time: 62.1 us; the launch traced here: 61.8 us
  Pallas kernels  58.4 us (94%)
  local copies, waits for them, and re-layouts  2.75 us (4%)
  between operations  0.64 us (1%)
    pallas_call x1, Pallas kernels, local(): pl.pallas_call(functools.partial(kernel, dims), out_shape=(field, field),...  58.4 us
    unnamed x2, local copies, waits for them, and re-layouts  2.75 us

profile of v2, /device:TPU:1, one launch (start us, length us, event | category | flops | bytes accessed | tf_op | source)
XLA Modules:
  0.0 61.8 jit_solution(14399170363218239252)
XLA Ops:
  0.6 58.4 %stress_two_steps.1 = (f32[2,4096]{1,0:T(2,128)}, f32[2,4096]{1,0:T(2,128)}) custom-call(s32[16]{0:T(128)} %home.1, s32[3,384]{1,0:T(4,128)} %far.1, s32[3,64]{1,0:T(4,128)} %near_list.1, bf16[2,4096]{1,0:T(2,128)(2,1)} %slip.1, f32[2,4096]{1,0:T(2,128)} %effect.1, bf16[12288,256]{1,0:T(8,128)(2,1)} %bitcast.4, bf16[12288,256]{1,0:T(8,128)(2,1)} %bitcast.5, ...), custom_call_target="tpu_custom_call" | custom-call | tf_op jit(solution)/shard_map/stress_two_steps/pallas_call | solution.py:390
  59.0 1.4 %copy.12 = f32[2,4096]{1,0:T(2,128)} copy(f32[2,4096]{1,0:T(2,128)} %get-tuple-element.4) | data formatting | bytes 65536
  60.4 1.4 %copy.13 = f32[2,4096]{1,0:T(2,128)} copy(f32[2,4096]{1,0:T(2,128)} %get-tuple-element.5) | data formatting | bytes 65536

commit v3 on v2

v3 whole, which is shorter than its diff:
```python
import functools
import itertools

import jax
import jax.numpy as jnp
from jax import lax
from jax.experimental import pallas as pl
from jax.experimental.pallas import tpu as pltpu
from jax.sharding import PartitionSpec as P

AXES = ("wide", "narrow")
MESH = pl.DeviceIdType.MESH
BF = jnp.bfloat16
F32 = jnp.float32
I32 = jnp.int32
WORD_HALF = 1 << 16
NO_BLOCK = 32767


def dot_nt(a, b):
    return lax.dot_general(a, b, (((1,), (1,)), ((), ())), preferred_element_type=F32)


def dot_nn(a, b):
    return lax.dot_general(a, b, (((1,), (0,)), ((), ())), preferred_element_type=F32)


def hot(mask):
    return jnp.where(mask, 1.0, 0.0).astype(BF)


def iota(shape, dim):
    return lax.broadcasted_iota(I32, shape, dim)


def near_first(extents):
    def hops(shift):
        return sum(min(d, n - d) for d, n, core in zip(shift, extents, (0, 1, 0, 0)) if not core)

    shifts = sorted(itertools.product(*map(range, extents)), key=hops)
    back = [shifts.index(tuple(-d % n for d, n in zip(s, extents))) for s in shifts]
    return shifts, back


def over(x, n):
    return x >> (n.bit_length() - 1)


def within(x, n):
    return x & (n - 1)


def rows_at(start, size):
    return pl.ds(pl.multiple_of(start, size), size)


def kernel(
    dims,
    home_hbm, far_hbm, near_list_hbm, slip_hbm, effect_hbm, u_hbm, v_hbm, near_hbm,
    first_hbm, second_hbm,
    home, far, near_list, slip, effect, first_out, second_out,
    u, v, near, index, pair_hot, slot_val, tri, tri_t, far_col, slot_hot, row_sel, row_sel_t,
    near_cols, near_rows, near_left, near_high, near_low, col_sel, col_sel_t, reply_sel, reply_sel_t, rep,
    left, mid, terms, terms_low, flat,
    sent, got, field, scale,
    small_sem, out_sem, load_sem, index_send, index_recv, send_sem, recv_sem,
):
    wide_n, narrow_n, nb, cap, adm, near_n, block, rank = dims
    devices = wide_n * narrow_n
    tiles = adm // 8
    cols2 = 2 * adm
    per = 2 * cap
    index_rows = index.shape[1]
    col_rows = -(-adm // 128)
    half = block // 2
    my_wide = lax.axis_index("wide")
    my_narrow = lax.axis_index("narrow")

    lists = [
        pltpu.make_async_copy(home_hbm, home, small_sem.at[0]),
        pltpu.make_async_copy(far_hbm, far, small_sem.at[1]),
        pltpu.make_async_copy(near_list_hbm, near_list, small_sem.at[2]),
        pltpu.make_async_copy(slip_hbm, slip, small_sem.at[3]),
        pltpu.make_async_copy(effect_hbm, effect, small_sem.at[4]),
    ]
    for load in lists:
        load.start()
    wide_y, wide_c = wide_n // 2, 2
    narrow_x = 4 if narrow_n % 4 == 0 and narrow_n > 4 else 2
    narrow_z = narrow_n // narrow_x
    shifted_wide = {
        (dy, dc): lax.rem(my_wide // wide_c + dy, wide_y) * wide_c + lax.rem(my_wide % wide_c + dc, wide_c)
        for dy in range(wide_y)
        for dc in range(wide_c)
    }
    shifted_narrow = {
        (dx, dz): lax.rem(my_narrow // narrow_z + dx, narrow_x) * narrow_z
        + lax.rem(my_narrow % narrow_z + dz, narrow_z)
        for dx in range(narrow_x)
        for dz in range(narrow_z)
    }
    shifts, back = near_first((wide_y, wide_c, narrow_x, narrow_z))
    device_at = [(shifted_wide[dy, dc], shifted_narrow[dx, dz]) for dy, dc, dx, dz in shifts]
    far_to_near = range(devices - 1, 0, -1)
    group = devices // 2
    part = min(32, group)

    barrier = pltpu.get_barrier_semaphore()
    for p in far_to_near:
        pl.semaphore_signal(barrier, inc=1, device_id=device_at[p], device_id_type=MESH)

    loads = [
        pltpu.make_async_copy(u_hbm, u, load_sem.at[0]),
        pltpu.make_async_copy(v_hbm, v, load_sem.at[1]),
        pltpu.make_async_copy(near_hbm, near, load_sem.at[2]),
    ]
    for load in loads:
        load.start()

    for load in lists:
        load.wait()

    far_cols = far[1:2, :]
    rows = []
    for r in range(col_rows):
        width = min(128, adm - r * 128)
        piece = far_cols[:, r * 128 : r * 128 + width]
        if width < 128:
            piece = jnp.concatenate([piece, jnp.full((1, 128 - width), NO_BLOCK, I32)], axis=1)
        rows.append(piece)
    lane = iota((1, 128), 1)
    home_row = jnp.full((1, 128), NO_BLOCK, I32)
    for s in range(nb):
        home_row = jnp.where(lane == s, home[s], home_row)
    rows += [jnp.full((1, 128), NO_BLOCK, I32)] * (2 * index_rows - col_rows - 1) + [home_row]
    for r in range(index_rows):
        index[0, r : r + 1, :] = rows[r] + rows[index_rows + r] * WORD_HALF

    def index_row(start, size, r):
        word = index[start : start + size, r % index_rows, :]
        return word >> 16 if r >= index_rows else word & (WORD_HALF - 1)

    pl.semaphore_wait(barrier, devices - 1)
    for p in range(1, devices):
        pltpu.make_async_remote_copy(
            src_ref=index.at[0], dst_ref=index.at[back[p]],
            send_sem=index_send, recv_sem=index_recv.at[back[p] // group],
            device_id=device_at[p], device_id_type=MESH,
        ).start()

    row_slot = jnp.zeros((1, adm), I32)
    near_row = jnp.zeros((1, near_n), I32)
    near_col = jnp.zeros((1, near_n), I32)
    far_rows = far[0:1, :]
    for s in range(nb):
        row_slot = jnp.where(far_rows == home[s], s, row_slot)
        near_row = jnp.where(near_list[0:1, :] == home[s], s, near_row)
        near_col = jnp.where(near_list[1:2, :] == home[s], s, near_col)
    place = iota((cols2, adm), 0)
    slot_hot[...] = hot(over(place, 16) * 8 + within(place, 8) == far[2:3, :])
    row_hot = hot(row_slot == within(iota((2 * nb, adm), 0), nb))
    pick = dot_nt(slot_hot[...], row_hot)
    comp = within(over(iota((cols2, 2 * nb), 0), 8), 2)
    row_sel[...] = jnp.where(comp == over(iota((cols2, 2 * nb), 1), nb), pick, 0.0).astype(BF)
    pick_t = dot_nt(row_hot, slot_hot[...])
    comp_t = within(over(iota((2 * nb, cols2), 1), 8), 2)
    row_sel_t[...] = jnp.where(comp_t == over(iota((2 * nb, cols2), 0), nb), pick_t, 0.0).astype(BF)
    tri[...] = hot(iota((adm, adm), 0) < iota((adm, adm), 1))
    tri_t[...] = hot(iota((adm, adm), 0) > iota((adm, adm), 1))
    col_ids = jnp.concatenate([far_cols.astype(F32), jnp.zeros((7, adm), F32)], axis=0).T
    far_col[...] = jnp.broadcast_to(col_ids[:, 0:1].astype(I32), (adm, devices))

    near_place = iota((2 * near_n, near_n), 0)
    near_hot = hot(over(near_place, 16) * 8 + within(near_place, 8) == near_list[2:3, :])
    block_of = within(iota((2 * nb, near_n), 0), nb)
    near_pick = dot_nt(near_hot, hot(near_col == block_of))
    comp = within(over(iota((2 * near_n, 2 * nb), 0), 8), 2)
    near_cols[...] = jnp.where(
        comp == over(iota((2 * near_n, 2 * nb), 1), nb), near_pick, 0.0
    ).astype(BF)
    near_pick_t = dot_nt(hot(near_row == block_of), near_hot)
    comp_t = within(over(iota((2 * nb, 2 * near_n), 1), 8), 2)
    near_rows[...] = jnp.where(
        comp_t == over(iota((2 * nb, 2 * near_n), 0), nb), near_pick_t, 0.0
    ).astype(BF)

    rep_rows = devices * per
    rep[...] = hot(over(iota((group * per, group), 0), per) == iota((group * per, group), 1))

    def by_block(ref):
        for c in range(2):
            for s in range(nb):
                piece = ref[c : c + 1, s * block : (s + 1) * block]
                field[c * nb + s : c * nb + s + 1, :] = piece.astype(F32)
        return field[...]

    def by_patch(value, ref):
        field[...] = value
        for c in range(2):
            for s in range(nb):
                ref[c : c + 1, s * block : (s + 1) * block] = field[c * nb + s : c * nb + s + 1, :]

    def wait_bytes(ref, sem):
        pltpu.make_async_copy(ref, ref, sem).wait()

    diag = within(iota((16, 8 * rank), 0), 8) == over(iota((16, 8 * rank), 1), rank)
    unroll = 16 if tiles % 16 == 0 else 1

    def over_tiles(step):
        def body(i, carry):
            for k in range(unroll):
                step(i * unroll + k)
            return carry

        lax.fori_loop(0, tiles // unroll, body, 0)

    def contract(factor):
        def step(t):
            y = dot_nt(left[rows_at(t * 16, 16), :], factor[rows_at(t * 8 * rank, 8 * rank), :])
            mid[rows_at(t * 16, 16), :] = jnp.where(diag, y, 0.0).astype(BF)

        over_tiles(step)

    def expand(factor, split):
        def step(t):
            y = dot_nn(mid[rows_at(t * 16, 16), :], factor[rows_at(t * 8 * rank, 8 * rank), :])
            high = y.astype(BF)
            terms[rows_at(t * 16, 16), :] = high
            if split:
                terms_low[rows_at(t * 16, 16), :] = (y - high.astype(F32)).astype(BF)

        over_tiles(step)

    def exchange(n, sel, right, order):
        for i in order:
            y = dot_nn(sel[i * part * per : (i + 1) * part * per, :], right)
            y = y.reshape(part, per, block)
            y = jnp.concatenate([y[:, :, :half], y[:, :, half:]], axis=1)
            sent[n, i * part : (i + 1) * part] = y.astype(BF)
            for p in range((i + 1) * part - 1, i * part - 1, -1):
                if p == 0:
                    got[n, 0] = sent[n, 0]
                    continue
                pltpu.make_async_remote_copy(
                    src_ref=sent.at[n, p], dst_ref=got.at[n, back[p]],
                    send_sem=send_sem.at[n], recv_sem=recv_sem.at[n],
                    device_id=device_at[p], device_id_type=MESH,
                ).start()

    parts = devices // part
    far_parts = range(parts - 1, -1, -1)

    def land(n):
        wait_bytes(got.at[n, pl.ds(0, devices - 1)], recv_sem.at[n])
        y = got[n].astype(F32)
        y = jnp.concatenate([y[:, :per, :], y[:, per:, :]], axis=2)
        flat[...] = y.reshape(rep_rows, block).astype(BF)

    def send_rates(n, x, order):
        exchange(n, reply_sel, jnp.concatenate([x] * cap, axis=0), order)

    def near_part(x):
        near_left[...] = dot_nn(near_cols[...], x).astype(BF)
        which = within(iota((16, block), 0), 8)
        steps = 2 if near_n % 16 == 0 else 1

        def body(i, carry):
            for k in range(steps):
                t = i * steps + k
                x_tile = near_left[rows_at(t * 16, 16), :]
                y = jnp.zeros((16, block), F32)
                for j in range(8):
                    term = dot_nt(x_tile, near[pl.ds(pl.multiple_of((t * 8 + j) * block, block), block), :])
                    y = jnp.where(which == j, term, y)
                high = y.astype(BF)
                near_high[rows_at(t * 16, 16), :] = high
                near_low[rows_at(t * 16, 16), :] = (y - high.astype(F32)).astype(BF)
            return carry

        lax.fori_loop(0, near_n // (8 * steps), body, 0)
        return dot_nn(near_rows[...], near_high[...]) + dot_nn(near_rows[...], near_low[...])

    def row_rates(x):
        left[...] = dot_nn(row_sel[...], x).astype(BF)

    def send_back(n):
        exchange(n, col_sel_t, terms[...], far_parts)

    def finish(n_rates, n_back, total):
        land(n_rates)
        left[...] = dot_nn(col_sel[...], flat[...]).astype(BF)
        contract(v)
        expand(u, True)
        total = total + dot_nn(row_sel_t[...], terms[...])
        total = total + dot_nn(row_sel_t[...], terms_low[...])
        land(n_back)
        return total + dot_nn(reply_sel_t[...], flat[...])

    scale[...] = by_block(effect)
    x = by_block(slip).astype(BF)
    row_rates(x)
    loads[0].wait()
    contract(u)

    loads[1].wait()
    expand(v, False)

    lanes = 2 * nb * cap
    lane_k = over(iota((group, lanes), 1), 2 * nb)
    lane_s = within(iota((group, lanes), 1), nb) + 1
    reply_mask = within(iota((group * per, lanes), 0), per) == over(iota((group * per, lanes), 1), nb)
    for h in range(2):
        wait_bytes(index.at[pl.ds(0, group - 1 + h)], index_recv.at[h])
        first_of, end = h * group, (h + 1) * group
        for q in range(first_of, end, part):
            wanted = jnp.concatenate(
                [index_row(q, part, r) for r in range(col_rows)], axis=1
            )[:, :adm]
            val = jnp.zeros((part, adm), F32)
            for s in range(nb):
                val = jnp.where(wanted == home[s], float(s + 1), val)
            slot_val[q : q + part, :] = val
            pair_hot[q : q + part, :] = hot(val > 0.0)
        ranks = dot_nn(pair_hot[first_of:end, :], tri[...])
        chosen = jnp.zeros((group, lanes), F32)
        for k in range(cap):
            slot_k = jnp.sum(
                jnp.where(ranks == float(k), slot_val[first_of:end, :], 0.0), axis=1, keepdims=True
            )
            chosen = jnp.where(lane_k == k, slot_k, chosen)
        wants = jnp.where(chosen == lane_s.astype(F32), 1.0, 0.0)
        spread = dot_nn(rep[...], wants.astype(BF))
        reply_sel[first_of * per : end * per, :] = jnp.where(reply_mask, spread, 0.0).astype(BF)
        send_rates(0, x, range(h * parts // 2, (h + 1) * parts // 2))

    homes = index_row(0, devices, 2 * index_rows - 1).astype(F32).T.astype(I32)
    tall = 128 if adm % 128 == 0 else adm
    founds = []
    for q in range(0, adm, tall):
        ids = far_col[q : q + tall, :]
        found = jnp.zeros((tall, devices), F32)
        for s in range(nb):
            found = jnp.where(ids == homes[s : s + 1, :], 1.0, found)
        founds.append(found.astype(BF))
    found = jnp.concatenate(founds, axis=0)
    place_in = (dot_nn(tri_t[...], found) * found.astype(F32)).astype(BF)
    owner = dot_nt(iota((8, devices), 1).astype(BF), found)
    place_in = dot_nt(jnp.ones((8, devices), BF), place_in)
    both = jnp.concatenate([owner[0:1], place_in[0:1], jnp.zeros((6, adm), F32)], axis=0).astype(BF)
    to_row = dot_nt(both, slot_hot[...])
    to_row = (to_row[0:1] * per + to_row[1:2] * 2).astype(I32)
    to_row = to_row + within(over(iota((1, cols2), 1), 8), 2)
    band = min(128, rep_rows)

    def rows_body(i, carry):
        col_sel_t[rows_at(i * band, band), :] = hot(iota((band, cols2), 0) == to_row - i * band)
        return carry

    lax.fori_loop(0, rep_rows // band, rows_body, 0)
    send_back(1)

    side = 256 if cols2 % 256 == 0 else cols2

    for i in range(0, rep_rows, band):
        for k in range(0, cols2, side):
            col_sel[k : k + side, i : i + band] = col_sel_t[i : i + band, k : k + side].T

    fold = hot(within(iota((2 * nb, lanes), 1), 2 * nb) == iota((2 * nb, lanes), 0))
    reply_sel_t[...] = dot_nt(fold, reply_sel[...]).astype(BF)

    loads[2].wait()
    first = finish(0, 1, near_part(x))
    x = (x.astype(F32) * jnp.exp(jnp.tanh(first / scale[...]))).astype(BF)
    send_rates(2, x, far_parts)
    by_patch(first, first_out)
    first_copy = pltpu.make_async_copy(first_out, first_hbm, out_sem.at[0])
    first_copy.start()
    row_rates(x)
    contract(u)
    expand(v, False)
    send_back(3)
    by_patch(finish(2, 3, near_part(x)), second_out)
    second_copy = pltpu.make_async_copy(second_out, second_hbm, out_sem.at[1])
    second_copy.start()

    wait_bytes(index.at[pl.ds(0, devices - 1)], index_send)
    first_copy.wait()
    second_copy.wait()
    for n in range(4):
        wait_bytes(sent.at[n, pl.ds(0, devices - 1)], send_sem.at[n])


def hand_out(first_in, second_in, first_out, second_out):
    first_out[...] = first_in[...]
    second_out[...] = second_in[...]


def local(slip, effect_stress, home_blocks, far_list, u_factor, v_factor, near_list, near_block):
    wide_n, narrow_n = lax.axis_size("wide"), lax.axis_size("narrow")
    devices = wide_n * narrow_n
    nb = home_blocks.shape[0]
    block = slip.shape[1] // nb
    adm, rank, _ = u_factor.shape
    near_n = near_list.shape[1]
    cap = max(2, adm // devices + 1)
    per = 2 * cap
    rep_rows = devices * per
    cols2 = 2 * adm
    index_rows = (-(-adm // 128) + 2) // 2
    dims = (wide_n, narrow_n, nb, cap, adm, near_n, block, rank)
    vmem = pl.BlockSpec(memory_space=pltpu.VMEM)
    hbm = pl.BlockSpec(memory_space=pl.ANY)
    field = jax.ShapeDtypeStruct((2, nb * block), F32)
    dma = pltpu.SemaphoreType.DMA
    results = pl.pallas_call(
        functools.partial(kernel, dims),
        out_shape=(field, field),
        in_specs=[hbm] * 8,
        out_specs=(hbm, hbm),
        scratch_shapes=[
            pltpu.SMEM(home_blocks.shape, I32),
            pltpu.VMEM(far_list.shape, I32),
            pltpu.VMEM(near_list.shape, I32),
            pltpu.VMEM(slip.shape, BF),
            pltpu.VMEM(slip.shape, F32),
            pltpu.VMEM(slip.shape, F32),
            pltpu.VMEM(slip.shape, F32),
            pltpu.VMEM((adm * rank, block), BF),
            pltpu.VMEM((adm * rank, block), BF),
            pltpu.VMEM((near_n * block, block), BF),
            pltpu.VMEM((devices, index_rows, 128), I32),
            pltpu.VMEM((devices, adm), BF),
            pltpu.VMEM((devices, adm), F32),
            pltpu.VMEM((adm, adm), BF),
            pltpu.VMEM((adm, adm), BF),
            pltpu.VMEM((adm, devices), I32),
            pltpu.VMEM((cols2, adm), BF),
            pltpu.VMEM((cols2, 2 * nb), BF),
            pltpu.VMEM((2 * nb, cols2), BF),
            pltpu.VMEM((2 * near_n, 2 * nb), BF),
            pltpu.VMEM((2 * nb, 2 * near_n), BF),
            pltpu.VMEM((2 * near_n, block), BF),
            pltpu.VMEM((2 * near_n, block), BF),
            pltpu.VMEM((2 * near_n, block), BF),
            pltpu.VMEM((cols2, rep_rows), BF),
            pltpu.VMEM((rep_rows, cols2), BF),
            pltpu.VMEM((rep_rows, 2 * nb * cap), BF),
            pltpu.VMEM((2 * nb, rep_rows), BF),
            pltpu.VMEM((rep_rows // 2, devices // 2), BF),
            pltpu.VMEM((cols2, block), BF),
            pltpu.VMEM((cols2, 8 * rank), BF),
            pltpu.VMEM((cols2, block), BF),
            pltpu.VMEM((cols2, block), BF),
            pltpu.VMEM((rep_rows, block), BF),
            pltpu.VMEM((4, devices, 2 * per, block // 2), BF),
            pltpu.VMEM((4, devices, 2 * per, block // 2), BF),
            pltpu.VMEM((2 * nb, block), F32),
            pltpu.VMEM((2 * nb, block), F32),
            dma((5,)),
            dma((2,)),
            dma((3,)),
            dma(()),
            dma((2,)),
            dma((4,)),
            dma((4,)),
        ],
        compiler_params=pltpu.CompilerParams(
            collective_id=0, has_side_effects=True, vmem_limit_bytes=56 << 20
        ),
        name="stress_two_steps",
    )(
        home_blocks,
        far_list,
        near_list,
        slip,
        effect_stress,
        u_factor.reshape(adm * rank, block),
        v_factor.reshape(adm * rank, block),
        near_block.reshape(near_n * block, block),
    )
    return pl.pallas_call(
        hand_out,
        out_shape=(field, field),
        in_specs=[vmem, vmem],
        out_specs=(vmem, vmem),
        name="hand_out",
    )(*results)


def solution(mesh):
    in_specs = (
        P(None, AXES),
        P(None, AXES),
        P(AXES),
        P(None, AXES),
        P(AXES, None, None),
        P(AXES, None, None),
        P(None, AXES),
        P(AXES, None, None),
    )
    out_specs = (P(None, AXES), P(None, AXES))
    return jax.shard_map(local, mesh=mesh, in_specs=in_specs, out_specs=out_specs, check_vma=False)
```

time: 62.1 us -> 52.5 us (0.85)
  Pallas kernels: 58.4 us -> 51.7 us
  local copies, waits for them, and re-layouts: 2.75 us -> 0 us
    pallas_call x1, Pallas kernels: 58.4 us -> 50.3 us  [local(): pl.pallas_call(functools.partial(kernel, dims), out_shape=(field, field),...]
    unnamed x2 -> x0, local copies, waits for them, and re-layouts: 2.75 us -> none
    pallas_call x0 -> x1, Pallas kernels: none -> 1.4 us  [local(): pl.pallas_call(hand_out, out_shape=(field, field), in_specs=[vmem, vmem],...]
where the time goes in v3:
time: 52.5 us; the launch traced here: 52.3 us
  Pallas kernels  51.7 us (98%)
  between operations  0.64 us (1%)
    pallas_call x1, Pallas kernels, local(): pl.pallas_call(functools.partial(kernel, dims), out_shape=(field, field),...  50.3 us
    pallas_call x1, Pallas kernels, local(): pl.pallas_call(hand_out, out_shape=(field, field), in_specs=[vmem, vmem],...  1.4 us

profile of v3, /device:TPU:1, one launch (start us, length us, event | category | flops | bytes accessed | tf_op | source)
XLA Modules:
  0.0 52.3 jit_solution(8018579849712979095)
XLA Ops:
  0.6 50.3 %stress_two_steps.1 = (f32[2,4096]{1,0:T(2,128)}, f32[2,4096]{1,0:T(2,128)}) custom-call(s32[16]{0:T(128)} %home_hbm.1, s32[3,384]{1,0:T(4,128)} %far_hbm.1, s32[3,64]{1,0:T(4,128)} %near_list_hbm.1, bf16[2,4096]{1,0:T(2,128)(2,1)} %slip_hbm.1, f32[2,4096]{1,0:T(2,128)} %effect_hbm.1, bf16[12288,256]{1,0:T(8,128)(2,1)} %bitcast.4, ...), custom_call_target="tpu_custom_call" | custom-call | tf_op jit(solution)/shard_map/stress_two_steps/pallas_call | solution.py:415
  50.9 1.4 %hand_out.1 = (f32[2,4096]{1,0:T(2,128)}, f32[2,4096]{1,0:T(2,128)}) custom-call(f32[2,4096]{1,0:T(2,128)} %get-tuple-element.4.first_in, f32[2,4096]{1,0:T(2,128)} %get-tuple-element.5.second_in), custom_call_target="tpu_custom_call" | custom-call | tf_op jit(solution)/shard_map/hand_out/pallas_call | solution.py:481

commit v4 on v3

--- a/solution.py
+++ b/solution.py
@@ -204,7 +204,7 @@
         pltpu.make_async_copy(ref, ref, sem).wait()
 
     diag = within(iota((16, 8 * rank), 0), 8) == over(iota((16, 8 * rank), 1), rank)
-    unroll = 16 if tiles % 16 == 0 else 1
+    unroll = 24 if tiles % 24 == 0 else 1
 
     def over_tiles(step):
         def body(i, carry):
@@ -231,7 +231,15 @@
 
         over_tiles(step)
 
-    def exchange(n, sel, right, order):
+    def send(n, p):
+        pltpu.make_async_remote_copy(
+            src_ref=sent.at[n, p], dst_ref=got.at[n, back[p]],
+            send_sem=send_sem.at[n], recv_sem=recv_sem.at[n],
+            device_id=device_at[p], device_id_type=MESH,
+        ).start()
+
+    def exchange(n, sel, right, order, later=False):
+        left_over = []
         for i in order:
             y = dot_nn(sel[i * part * per : (i + 1) * part * per, :], right)
             y = y.reshape(part, per, block)
@@ -240,12 +248,15 @@
             for p in range((i + 1) * part - 1, i * part - 1, -1):
                 if p == 0:
                     got[n, 0] = sent[n, 0]
-                    continue
-                pltpu.make_async_remote_copy(
-                    src_ref=sent.at[n, p], dst_ref=got.at[n, back[p]],
-                    send_sem=send_sem.at[n], recv_sem=recv_sem.at[n],
-                    device_id=device_at[p], device_id_type=MESH,
-                ).start()
+                elif later:
+                    left_over.append((n, p))
+                else:
+                    send(n, p)
+        return left_over
+
+    def send_share(waiting, done, steps):
+        for n, p in waiting[len(waiting) * done // steps : len(waiting) * (done + 1) // steps]:
+            send(n, p)
 
     parts = devices // part
     far_parts = range(parts - 1, -1, -1)
@@ -256,35 +267,29 @@
         y = jnp.concatenate([y[:, :per, :], y[:, per:, :]], axis=2)
         flat[...] = y.reshape(rep_rows, block).astype(BF)
 
-    def send_rates(n, x, order):
-        exchange(n, reply_sel, jnp.concatenate([x] * cap, axis=0), order)
-
-    def near_part(x):
+    def send_rates(n, x, order, later=False):
+        return exchange(n, reply_sel, jnp.concatenate([x] * cap, axis=0), order, later)
+
+    def near_part(x, waiting):
         near_left[...] = dot_nn(near_cols[...], x).astype(BF)
         which = within(iota((16, block), 0), 8)
-        steps = 2 if near_n % 16 == 0 else 1
-
-        def body(i, carry):
-            for k in range(steps):
-                t = i * steps + k
-                x_tile = near_left[rows_at(t * 16, 16), :]
-                y = jnp.zeros((16, block), F32)
-                for j in range(8):
-                    term = dot_nt(x_tile, near[pl.ds(pl.multiple_of((t * 8 + j) * block, block), block), :])
-                    y = jnp.where(which == j, term, y)
-                high = y.astype(BF)
-                near_high[rows_at(t * 16, 16), :] = high
-                near_low[rows_at(t * 16, 16), :] = (y - high.astype(F32)).astype(BF)
-            return carry
-
-        lax.fori_loop(0, near_n // (8 * steps), body, 0)
+        for t in range(near_n // 8):
+            x_tile = near_left[t * 16 : (t + 1) * 16, :]
+            y = jnp.zeros((16, block), F32)
+            for j in range(8):
+                g = t * 8 + j
+                y = jnp.where(which == j, dot_nt(x_tile, near[g * block : (g + 1) * block, :]), y)
+                send_share(waiting, g, near_n)
+            high = y.astype(BF)
+            near_high[t * 16 : (t + 1) * 16, :] = high
+            near_low[t * 16 : (t + 1) * 16, :] = (y - high.astype(F32)).astype(BF)
         return dot_nn(near_rows[...], near_high[...]) + dot_nn(near_rows[...], near_low[...])
 
     def row_rates(x):
         left[...] = dot_nn(row_sel[...], x).astype(BF)
 
     def send_back(n):
-        exchange(n, col_sel_t, terms[...], far_parts)
+        return exchange(n, col_sel_t, terms[...], far_parts, True)
 
     def finish(n_rates, n_back, total):
         land(n_rates)
@@ -357,7 +362,9 @@
         return carry
 
     lax.fori_loop(0, rep_rows // band, rows_body, 0)
-    send_back(1)
+    waiting = send_back(1)
+    loads[2].wait()
+    near_sum = near_part(x, waiting)
 
     side = 256 if cols2 % 256 == 0 else cols2
 
@@ -368,8 +375,7 @@
     fold = hot(within(iota((2 * nb, lanes), 1), 2 * nb) == iota((2 * nb, lanes), 0))
     reply_sel_t[...] = dot_nt(fold, reply_sel[...]).astype(BF)
 
-    loads[2].wait()
-    first = finish(0, 1, near_part(x))
+    first = finish(0, 1, near_sum)
     x = (x.astype(F32) * jnp.exp(jnp.tanh(first / scale[...]))).astype(BF)
     send_rates(2, x, far_parts)
     by_patch(first, first_out)
@@ -378,8 +384,8 @@
     row_rates(x)
     contract(u)
     expand(v, False)
-    send_back(3)
-    by_patch(finish(2, 3, near_part(x)), second_out)
+    waiting = send_back(3)
+    by_patch(finish(2, 3, near_part(x, waiting)), second_out)
     second_copy = pltpu.make_async_copy(second_out, second_hbm, out_sem.at[1])
     second_copy.start()
 

time: 52.5 us -> 51.6 us (0.983)
  Pallas kernels: 51.7 us -> 50.7 us
    pallas_call x1, Pallas kernels: 50.3 us -> 49.3 us  [local(): pl.pallas_call(functools.partial(kernel, dims), out_shape=(field, field),...]
where the time goes in v4:
time: 51.6 us; the launch traced here: 51.4 us
  Pallas kernels  50.7 us (98%)
  between operations  0.64 us (1%)
    pallas_call x1, Pallas kernels, local(): pl.pallas_call(functools.partial(kernel, dims), out_shape=(field, field),...  49.3 us
    pallas_call x1, Pallas kernels, local(): pl.pallas_call(hand_out, out_shape=(field, field), in_specs=[vmem, vmem],...  1.4 us

profile of v4, /device:TPU:1, one launch (start us, length us, event | category | flops | bytes accessed | tf_op | source)
XLA Modules:
  0.0 51.4 jit_solution(7239563531557565340)
XLA Ops:
  0.6 49.3 %stress_two_steps.1 = (f32[2,4096]{1,0:T(2,128)}, f32[2,4096]{1,0:T(2,128)}) custom-call(s32[16]{0:T(128)} %home_hbm.1, s32[3,384]{1,0:T(4,128)} %far_hbm.1, s32[3,64]{1,0:T(4,128)} %near_list_hbm.1, bf16[2,4096]{1,0:T(2,128)(2,1)} %slip_hbm.1, f32[2,4096]{1,0:T(2,128)} %effect_hbm.1, bf16[12288,256]{1,0:T(8,128)(2,1)} %bitcast.4, ...), custom_call_target="tpu_custom_call" | custom-call | tf_op jit(solution)/shard_map/stress_two_steps/pallas_call | solution.py:421
  50.0 1.4 %hand_out.1 = (f32[2,4096]{1,0:T(2,128)}, f32[2,4096]{1,0:T(2,128)}) custom-call(f32[2,4096]{1,0:T(2,128)} %get-tuple-element.4.first_in, f32[2,4096]{1,0:T(2,128)} %get-tuple-element.5.second_in), custom_call_target="tpu_custom_call" | custom-call | tf_op jit(solution)/shard_map/hand_out/pallas_call | solution.py:487

commit v5 on v4

--- a/solution.py
+++ b/solution.py
@@ -103,7 +103,7 @@
     device_at = [(shifted_wide[dy, dc], shifted_narrow[dx, dz]) for dy, dc, dx, dz in shifts]
     far_to_near = range(devices - 1, 0, -1)
     group = devices // 2
-    part = min(32, group)
+    part = min(64, group)
 
     barrier = pltpu.get_barrier_semaphore()
     for p in far_to_near:
@@ -188,10 +188,10 @@
     rep[...] = hot(over(iota((group * per, group), 0), per) == iota((group * per, group), 1))
 
     def by_block(ref):
+        whole = ref[...].astype(F32)
         for c in range(2):
             for s in range(nb):
-                piece = ref[c : c + 1, s * block : (s + 1) * block]
-                field[c * nb + s : c * nb + s + 1, :] = piece.astype(F32)
+                field[c * nb + s : c * nb + s + 1, :] = whole[c : c + 1, s * block : (s + 1) * block]
         return field[...]
 
     def by_patch(value, ref):

time: 51.6 us -> 51 us (0.988)
    pallas_call x1, Pallas kernels: 49.3 us -> 48.8 us  [local(): pl.pallas_call(functools.partial(kernel, dims), out_shape=(field, field),...]
where the time goes in v5:
time: 51 us; the launch traced here: 50.9 us
  Pallas kernels  50.2 us (98%)
  between operations  0.64 us (1%)
    pallas_call x1, Pallas kernels, local(): pl.pallas_call(functools.partial(kernel, dims), out_shape=(field, field),...  48.8 us
    pallas_call x1, Pallas kernels, local(): pl.pallas_call(hand_out, out_shape=(field, field), in_specs=[vmem, vmem],...  1.4 us

profile of v5, /device:TPU:1, one launch (start us, length us, event | category | flops | bytes accessed | tf_op | source)
XLA Modules:
  0.0 50.9 jit_solution(8965098844575974108)
XLA Ops:
  0.6 48.8 %stress_two_steps.1 = (f32[2,4096]{1,0:T(2,128)}, f32[2,4096]{1,0:T(2,128)}) custom-call(s32[16]{0:T(128)} %home_hbm.1, s32[3,384]{1,0:T(4,128)} %far_hbm.1, s32[3,64]{1,0:T(4,128)} %near_list_hbm.1, bf16[2,4096]{1,0:T(2,128)(2,1)} %slip_hbm.1, f32[2,4096]{1,0:T(2,128)} %effect_hbm.1, bf16[12288,256]{1,0:T(8,128)(2,1)} %bitcast.4, ...), custom_call_target="tpu_custom_call" | custom-call | tf_op jit(solution)/shard_map/stress_two_steps/pallas_call | solution.py:421
  49.4 1.4 %hand_out.1 = (f32[2,4096]{1,0:T(2,128)}, f32[2,4096]{1,0:T(2,128)}) custom-call(f32[2,4096]{1,0:T(2,128)} %get-tuple-element.4.first_in, f32[2,4096]{1,0:T(2,128)} %get-tuple-element.5.second_in), custom_call_target="tpu_custom_call" | custom-call | tf_op jit(solution)/shard_map/hand_out/pallas_call | solution.py:487
